TPU v7x, 32 devices: a whole 2x2x4 slice. The times are simulated.
32 devices in a mesh: clip: 8 (over z, y), frame: 4 (over x, core).
Axes of the slice: x: 2, y: 2, z: 4, core: 2. Of those that a mesh axis runs over, the one named last changes fastest.
Arguments:
- frames: bfloat16 [256, 16, 1152], P('clip', 'frame'), may hold values from -6 to 6
- conv_weight: bfloat16 [3, 1152, 1152], replicated, may hold values from -0.109375 to 0.109375
- captions: bfloat16 [256, 1152], P(('clip', 'frame')), may hold values from -6 to 6
- positive: int32 [256], P('clip'), may hold values from 0 to 255, as said below
Outputs:
- loss: float32 [], replicated
- grad_weight: float32 [3, 1152, 1152], P(None, 'clip', 'frame')
- grad_captions: float32 [256, 1152], P(('clip', 'frame'))
Inputs may be any that keep to these rules, and one draw needn't show every extreme that they name: Each caption id is the positive of exactly one clip.
All inputs are finite; a program needn't handle non-finite values.
Results may differ from a plain program's by a relative error of at most 0.0028.
The roundings to bfloat16 on the way count: a program that leaves them out, or rounds other values in their place, can miss the bound.
Values may be sent and summed in bfloat16 or wider, within the bound.
A program may use at most 128 MiB of HBM per device.

v0:
```python
import jax
import jax.numpy as jnp
from jax import lax
from jax.sharding import PartitionSpec as P

FRAMES = 16


def with_halo(block, sides, width):
    for axis, dim in sides:
        count = lax.axis_size(axis)
        forward = [(i, i + 1) for i in range(count - 1)]
        backward = [(target, source) for source, target in forward]
        low = lax.ppermute(
            lax.slice_in_dim(block, block.shape[dim] - width, None, axis=dim), axis, forward
        )
        high = lax.ppermute(lax.slice_in_dim(block, 0, width, axis=dim), axis, backward)
        block = jnp.concatenate([low, block, high], axis=dim)
    return block


def on_device(frames, conv_weight, captions, positive):
    clip_dev, fr_dev, width = frames.shape
    rows = clip_dev * fr_dev
    padded = with_halo(frames, (("frame", 1),), 1)
    shifted = [padded[:, k : k + fr_dev].reshape(rows, width) for k in range(3)]
    conv = jnp.dot(shifted[0], conv_weight[0], preferred_element_type=jnp.float32)
    conv = conv + jnp.dot(shifted[1], conv_weight[1], preferred_element_type=jnp.float32)
    conv = conv + jnp.dot(shifted[2], conv_weight[2], preferred_element_type=jnp.float32)
    hidden = frames.reshape(rows, width).astype(jnp.float32) + jax.nn.gelu(conv)
    partial_pool = jnp.sum(hidden.reshape(clip_dev, fr_dev, width), axis=1)
    pooled = lax.psum(partial_pool, "frame") / FRAMES
    pnorm = jnp.sqrt(jnp.sum(pooled * pooled, axis=1, keepdims=True) + 1e-06)
    unit = pooled / pnorm
    u_low = unit.astype(jnp.bfloat16)
    capf = captions.astype(jnp.float32)
    cnorm = jnp.sqrt(jnp.sum(capf * capf, axis=1, keepdims=True) + 1e-06)
    vunit = capf / cnorm
    v_low = vunit.astype(jnp.bfloat16)
    cap_dev = captions.shape[0]
    frame_pos = lax.axis_index("frame")
    piece = lax.all_gather(v_low, "clip", axis=0, tiled=True)
    count = piece.shape[0]
    place = jnp.arange(count, dtype=jnp.int32)
    ids = place // cap_dev * clip_dev + frame_pos * cap_dev + place % cap_dev
    logits = (
        10.0
        * lax.dot_general(
            u_low, piece, (((1,), (1,)), ((), ())), preferred_element_type=jnp.float32
        )
        - 10.0
    )
    match = (positive[:, None] == ids[None, :]).astype(jnp.float32)
    sign = 2.0 * match - 1.0
    total = jnp.sum(jax.nn.softplus(-sign * logits))
    coef = (10.0 * (jax.nn.sigmoid(logits) - match)).astype(jnp.bfloat16)
    du_acc = jnp.dot(coef, piece, preferred_element_type=jnp.float32)
    dv_piece = lax.dot_general(
        coef, u_low, (((0,), (0,)), ((), ())), preferred_element_type=jnp.float32
    )
    total, du_part, dv_all = (total, du_acc, dv_piece)
    dv_mine = lax.psum_scatter(dv_all, "clip", scatter_dimension=0, tiled=True)
    grad_captions = (dv_mine - vunit * jnp.sum(vunit * dv_mine, axis=1, keepdims=True)) / cnorm
    loss = lax.psum(total, ("clip", "frame")) / (clip_dev * lax.axis_size("clip"))
    du_full = lax.psum(du_part, "frame")
    dpooled = (du_full - unit * jnp.sum(unit * du_full, axis=1, keepdims=True)) / pnorm
    dhidden = jnp.broadcast_to((dpooled / FRAMES)[:, None, :], (clip_dev, fr_dev, width)).reshape(
        rows, width
    )
    _, pull = jax.vjp(jax.nn.gelu, conv)
    dconv = pull(dhidden)[0].astype(jnp.bfloat16).reshape(clip_dev, fr_dev, width)
    dconv_cols = lax.all_to_all(dconv, "frame", split_axis=2, concat_axis=1, tiled=True)
    block = fr_dev + 2
    col_width = dconv_cols.shape[2]
    every_block = lax.all_gather(padded, "frame", axis=1, tiled=True)
    groups = every_block.shape[1] // block
    blocks = every_block.reshape(clip_dev, groups, block, width)
    grads = dconv_cols.reshape(clip_dev, groups, fr_dev, col_width)
    parts = [
        jnp.einsum(
            "cgtd,cgte->de", blocks[:, :, k : k + fr_dev], grads, preferred_element_type=jnp.float32
        )
        for k in range(3)
    ]
    terms = jnp.stack(parts)
    grad_weight = lax.psum_scatter(terms, "clip", scatter_dimension=1, tiled=True)
    return (loss, grad_weight, grad_captions)


def solution(mesh):
    placed = (P("clip", "frame", None), P(), P(("clip", "frame"), None), P("clip"))
    return jax.shard_map(
        on_device,
        mesh=mesh,
        in_specs=placed,
        out_specs=(P(), P(None, "clip", "frame"), P(("clip", "frame"), None)),
        check_vma=False,
    )
```

profile of v0, /device:TPU:0, one launch (start us, length us, event | category | flops | bytes accessed | tf_op | source)
XLA Modules:
  0.0 296.5 jit_solution(3612880796627355824)
XLA Ops:
  7.2 0.0 all-reduce.5.cloned.1.call-start
  7.2 1.0 copy.13
  8.2 0.0 copy-start.1
  8.2 2.5 collective-permute-start
  10.7 1.3 collective-permute-start.1
  12.0 1.0 reshape.69
  13.1 0.8 fusion.26
  13.9 0.8 fusion.40
  14.7 2.3 fusion.2
  17.1 0.1 copy.14
  17.2 0.1 copy.16
  17.4 0.7 pad_maximum_fusion.3
  18.0 0.1 reshape.70
  18.1 0.1 reshape.71
  18.2 2.3 fusion
  20.5 0.0 copy-start.4
  20.5 2.5 multiply_add_fusion
  23.0 0.2 reshape.72
  23.2 1.0 reduce_sum.54
  24.2 0.0 all-reduce.5.cloned.1.call-update
  24.2 0.0 all-reduce.7.cloned.1.call-start
  24.3 31.7 %all_gather.6 = bf16[64,1152]{1,0:T(8,128)(2,1)S(1)} all-gather(bf16[8,1152]{1,0:T(8,128)(2,1)S(1)} %fusion.40), channel_id=1, replica_groups=mesh['clip'=8,'frame'=4] {'clip'}, dimensions={0}, use_global_device_ids=true | all-gather | bytes 165888 | tf_op jit(solution)/shard_map/all_gather | solution.py:42
  56.0 3.7 %all-reduce.5.cloned.1.call-done = f32[32,1152]{1,0:T(8,128)} async-done(((f32[32,1152]{1,0:T(8,128)}), f32[32,1152]{1,0:T(8,128)}) %all-reduce.5.cloned.1.call-update) | async-done | bytes 147472 | tf_op jit(solution)/shard_map/psum | solution.py:32
  59.7 1.1 multiply_reduce_fusion.1
  60.8 1.8 fusion.36
  62.6 0.9 fusion.42
  63.5 0.0 all-reduce.7.cloned.1.call-update
  63.5 0.0 all-gather.2.cloned.1.call-start
  63.6 0.8 pad_maximum_fusion.1
  64.4 0.0 all-gather.2.cloned.1.call-update
  64.4 30.8 %all-reduce.7.cloned.1.call-done = f32[32,1152]{1,0:T(8,128)} async-done(((f32[32,1152]{1,0:T(8,128)}), f32[32,1152]{1,0:T(8,128)}) %all-reduce.7.cloned.1.call-update) | async-done | bytes 147472 | tf_op jit(solution)/shard_map/psum | solution.py:65
  95.2 1.1 multiply_reduce_fusion
  96.3 1.0 divide_multiply_fusion
  97.3 0.1 broadcast_in_dim.2
  97.4 0.2 reshape.74
  97.6 0.4 fusion.22
  98.0 0.1 reshape.75
  98.1 0.9 copy.18
  99.0 1.8 reshape.82
  100.8 3.5 %all-to-all-start = ((bf16[4,2,18432]{2,1,0:T(2,128)(2,1)}), bf16[4,2,18432]{2,1,0:T(2,128)(2,1)S(1)}, u32[]{:S(2)}, u32[]{:S(2)}) async-start(bf16[4,2,18432]{2,1,0:T(2,128)(2,1)} %reshape.82), calls=%async_computation | async-start | bytes 589824 | tf_op jit(solution)/shard_map/all_to_all | solution.py:72
  104.3 0.0 all-reduce.9.cloned.1.call-start
  104.3 1.0 fusion.27
  105.3 0.0 all-reduce.9.cloned.1.call-update
  105.3 0.0 reduce-scatter.4.cloned.1.call-start
  105.4 8.4 %all-to-all-done = bf16[4,2,18432]{2,1,0:T(2,128)(2,1)S(1)} async-done(((bf16[4,2,18432]{2,1,0:T(2,128)(2,1)}), bf16[4,2,18432]{2,1,0:T(2,128)(2,1)S(1)}, u32[]{:S(2)}, u32[]{:S(2)}) %all-to-all-start) | async-done | bytes 294944 | tf_op jit(solution)/shard_map/all_to_all | solution.py:72
  113.8 0.6 reshape.83
  114.3 0.7 copy.20
  115.1 6.5 %all-gather.2.cloned.1.call-done = bf16[32,24,1152]{2,0,1:T(8,128)(2,1)} async-done(((bf16[32,6,1152]{2,0,1:T(8,128)(2,1)}), bf16[32,24,1152]{2,0,1:T(8,128)(2,1)}) %all-gather.2.cloned.1.call-update) | async-done | bytes 1769488 | tf_op jit(solution)/shard_map/all_gather | solution.py:75
  121.6 2.0 convolution_bitcast_fusion.1
  123.6 0.6 convolution_bitcast_fusion
  124.2 0.6 convolution_bitcast_fusion.2
  124.8 2.3 pad_maximum_fusion
  127.1 8.6 %copy.27 = f32[3,1152,288]{2,0,1:T(4,128)} copy(f32[3,1152,288]{1,2,0:T(8,128)} %pad_maximum_fusion) | data formatting | bytes 7962624
  135.6 9.0 %reshape.79 = f32[1152,864]{1,0:T(8,128)} reshape(f32[1152,3,288]{2,1,0:T(4,128)} %bitcast.56) | data formatting | bytes 7962624
  144.6 0.0 reduce-scatter.4.cloned.1.call-update
  144.7 0.6 copy-done.5
  145.3 0.6 dynamic-slice
  146.5 39.7 %psum.22 = f32[]{:T(128)} all-reduce(f32[]{:T(128)} %get-tuple-element.18), channel_id=1, replica_groups=mesh['clip'=8,'frame'=4] {'clip','frame'}, use_global_device_ids=true, to_apply=%region_5.6 | all-reduce | flops 1 | bytes 8 | tf_op jit(solution)/shard_map/psum | solution.py:64
  186.8 8.9 %all-reduce.9.cloned.1.call-done = f32[64,1152]{1,0:T(8,128)} async-done(((f32[64,1152]{1,0:T(8,128)}), f32[64,1152]{1,0:T(8,128)}) %all-reduce.9.cloned.1.call-update) | async-done | bytes 294928
  195.7 1.0 multiply_reduce_fusion.2
  196.7 1.5 subtract_divide_fusion
  198.2 88.1 %reduce-scatter.4.cloned.1.call-done = f32[144,864]{1,0:T(8,128)} async-done(((f32[1152,864]{1,0:T(8,128)}), f32[144,864]{1,0:T(8,128)}) %reduce-scatter.4.cloned.1.call-update) | async-done | bytes 497680
  286.3 1.6 reshape.80
  287.9 0.9 copy.21
  (15 shorter events, 0.1 us)
Async XLA Ops:
  7.2 52.5 %all-reduce.5.cloned.1.call-start = ((), (), s32[]{:S(2)}) async-start(), calls=%async_computation.2 | async-start | bytes 294912 | tf_op jit(solution)/shard_map/psum | solution.py:32
  8.2 9.2 %copy-start.1 = (bf16[32,4,1152]{2,1,0:T(4,128)(2,1)S(1)}, bf16[32,4,1152]{2,1,0:T(4,128)(2,1)}, u32[]{:S(2)}) copy-start(bf16[32,4,1152]{2,1,0:T(4,128)(2,1)} %param.4) | copy-start | bytes 884740
  8.2 8.8 %collective-permute-start = (bf16[32,1,1152]{2,0,1:T(8,128)(2,1)S(1)}, bf16[32,1,1152]{2,0,1:T(8,128)(2,1)S(1)}, u32[]{:S(2)}, u32[]{:S(2)}) collective-permute-start(bf16[32,1,1152]{2,0,1:T(8,128)(2,1)S(1)} %get-tuple-element.14), channel_id=1, source_target_pairs={{0,1},{1,2},{2,3},{4,5},{5,6},{6,7},{8,9},{9,10},{10,11},{12,13},{... | collective-permute-start | bytes 221192 | tf_op jit(solution)/shard_map/ppermute | solution.py:14
  10.7 6.5 %collective-permute-start.1 = (bf16[32,1,1152]{2,0,1:T(8,128)(2,1)S(1)}, bf16[32,1,1152]{2,0,1:T(8,128)(2,1)S(1)}, u32[]{:S(2)}, u32[]{:S(2)}) collective-permute-start(bf16[32,1,1152]{2,0,1:T(8,128)(2,1)S(1)} %get-tuple-element.15), channel_id=1, source_target_pairs={{1,0},{2,1},{3,2},{5,4},{6,5},{7,6},{9,8},{10,9},{11,10},{13,12},{... | collective-permute-start | bytes 221192 | tf_op jit(solution)/shard_map/ppermute | solution.py:17
  20.5 40.3 %copy-start.4 = (s32[32]{0:T(128)S(1)}, s32[32]{0:T(128)}, u32[]{:S(2)}) copy-start(s32[32]{0:T(128)} %param.7) | copy-start | bytes 388
  24.2 71.0 %all-reduce.7.cloned.1.call-start = ((), (), s32[]{:S(2)}) async-start(), calls=%async_computation.4 | async-start | bytes 294912 | tf_op jit(solution)/shard_map/psum | solution.py:65
  59.7 35.5 %copy-start.2 = (f32[32,1152]{1,0:T(8,128)S(1)}, f32[32,1152]{1,0:T(8,128)}, u32[]{:S(2)}) copy-start(f32[32,1152]{1,0:T(8,128)} %all-reduce.5.cloned.1.call-done) | copy-start | bytes 442372
  63.5 58.1 %all-gather.2.cloned.1.call-start = ((), (), s32[]{:S(2)}) async-start(), calls=%async_computation.3 | async-start | bytes 2211840 | tf_op jit(solution)/shard_map/all_gather | solution.py:75
  100.8 13.0 %all-to-all-start = ((bf16[4,2,18432]{2,1,0:T(2,128)(2,1)}), bf16[4,2,18432]{2,1,0:T(2,128)(2,1)S(1)}, u32[]{:S(2)}, u32[]{:S(2)}) async-start(bf16[4,2,18432]{2,1,0:T(2,128)(2,1)} %reshape.82), calls=%async_computation | async-start | bytes 589824 | tf_op jit(solution)/shard_map/all_to_all | solution.py:72
  104.3 91.5 %all-reduce.9.cloned.1.call-start = ((), (), s32[]{:S(2)}) async-start(), calls=%async_computation.6 | async-start | bytes 589824
  105.3 181.0 %reduce-scatter.4.cloned.1.call-start = ((), (), s32[]{:S(2)}) async-start(), calls=%async_computation.5 | async-start | bytes 4644864
  121.6 2.0 copy-start
  144.6 0.7 copy-start.5
  144.6 51.1 %copy-start.3 = (bf16[8,1152]{1,0:T(8,128)(2,1)S(1)}, bf16[8,1152]{1,0:T(8,128)(2,1)}, u32[]{:S(2)}) copy-start(bf16[8,1152]{1,0:T(8,128)(2,1)} %param.6) | copy-start | bytes 55300
Sparse Core Ops, SparseCore 0:
  24.3 35.3 all-reduce.4
  63.6 31.4 all-reduce.6
  97.3 24.2 all-gather.1
  124.8 70.9 all-reduce.8
  199.6 86.7 reduce-scatter.3
where the time goes:
time: 298 us; the launch traced here: 296 us
  waiting for transfers between devices  147 us (49%)
  blocking collectives  71.4 us (24%)
  local copies, waits for them, and re-layouts  28.2 us (9%)
  between operations  16.5 us (6%)
  matrix products  14 us (5%)
  other arithmetic  12.5 us (4%)
  starting transfers between devices  7.44 us (2%)
    unnamed x7, waiting for transfers between devices  97.1 us
    psum x1, blocking collectives, on_device(): lax.psum(total, ('clip', 'frame')) / (clip_dev * lax.axis_size('clip'))  39.7 us
    all_gather x1, blocking collectives, on_device(): piece = lax.all_gather(v_low, 'clip', axis=0, tiled=True)  31.7 us
    psum x1, waiting for transfers between devices, on_device(): du_full = lax.psum(du_part, 'frame')  30.8 us
    unnamed x20, local copies, waits for them, and re-layouts  24.6 us
    all_to_all x1, waiting for transfers between devices, on_device(): lax.all_to_all(dconv, 'frame', split_axis=2, concat_axis=1, tiled=True)  8.38 us
    all_gather x1, waiting for transfers between devices, on_device(): every_block = lax.all_gather(padded, 'frame', axis=1, tiled=True)  6.55 us
  transfers between devices with their start and end apart: 8, of which 6 were waited for; matrix products, arithmetic and copies ran while one was open for 13% of the time, Pallas kernels for 0%

commit v1 on v0

--- a/solution.py
+++ b/solution.py
@@ -1,6 +1,11 @@
+import functools
+import math
+
 import jax
 import jax.numpy as jnp
 from jax import lax
+from jax.experimental import pallas as pl
+from jax.experimental.pallas import tpu as pltpu
 from jax.sharding import PartitionSpec as P
 
 FRAMES = 16
@@ -19,7 +24,7 @@
     return block
 
 
-def on_device(frames, conv_weight, captions, positive):
+def plain(frames, conv_weight, captions, positive):
     clip_dev, fr_dev, width = frames.shape
     rows = clip_dev * fr_dev
     padded = with_halo(frames, (("frame", 1),), 1)
@@ -87,6 +92,421 @@
     return (loss, grad_weight, grad_captions)
 
 
+MESH = pl.DeviceIdType.MESH
+
+
+def remote(src, dst, send_sem, recv_sem, device):
+    return pltpu.make_async_remote_copy(
+        src_ref=src,
+        dst_ref=dst,
+        send_sem=send_sem,
+        recv_sem=recv_sem,
+        device_id=device,
+        device_id_type=MESH,
+    )
+
+
+def nt_dot(a, b):
+    return lax.dot_general(a, b, (((1,), (1,)), ((), ())), preferred_element_type=jnp.float32)
+
+
+def ring_to_clip(r, count):
+    high = r // (count // 2)
+    return 2 * r + high * (2 * count - 1 - 4 * r)
+
+
+def fused_kernel(
+    C,
+    F,
+    frames_ref,
+    w_hbm,
+    cap_ref,
+    pos_ref,
+    loss_ref,
+    gw_ref,
+    gc_ref,
+    w_ref,
+    x_rows,
+    xt,
+    xu,
+    x3,
+    v32,
+    vb,
+    u32,
+    ub,
+    slope,
+    dt,
+    dbuf,
+    acc,
+    w_sem,
+    fr_send,
+    fr_recv,
+    v1_send,
+    v1_recv,
+    v2_send,
+    v2_recv,
+    x1_send,
+    x1_recv,
+    x2_send,
+    x2_recv,
+    u1_send,
+    u1_recv,
+    u2_send,
+    u2_recv,
+    da_send,
+    da_recv,
+    ring_send,
+    ring_recv,
+):
+    D = cap_ref.shape[1]
+    NB = cap_ref.shape[0]
+    T = FRAMES
+    ROWS = T * NB
+    part = ROWS // F
+    RC = D // C
+    CC = D // F
+    c = lax.axis_index("clip")
+    f = lax.axis_index("frame")
+    half = C // 2
+    z = c // 2
+    pos = z + (c - 2 * z) * (C - 1 - 2 * z)
+    right = ring_to_clip(lax.rem(pos + 1, C), C)
+    left = ring_to_clip(lax.rem(pos + C - 1, C), C)
+
+    w_copies = [pltpu.make_async_copy(w_hbm.at[k], w_ref.at[k], w_sem.at[k]) for k in range(3)]
+    for copy in w_copies:
+        copy.start()
+
+    def cpeer(d):
+        return lax.rem(c + d, C)
+
+    def fpeer(d):
+        return lax.rem(f + d, F)
+
+    barrier = pltpu.get_barrier_semaphore()
+    for d in range(1, C):
+        pl.semaphore_signal(barrier, inc=1, device_id=(cpeer(d), f), device_id_type=MESH)
+    for d in range(1, F):
+        pl.semaphore_signal(barrier, inc=1, device_id=(c, fpeer(d)), device_id_type=MESH)
+    pl.semaphore_wait(barrier, C + F - 2)
+
+    sends = []
+
+    def go(copy):
+        copy.start()
+        sends.append(copy)
+
+    for d in range(1, F):
+        go(
+            remote(
+                frames_ref.at[fpeer(d)],
+                x_rows.at[f],
+                fr_send.at[d],
+                fr_recv.at[d],
+                (c, fpeer(d)),
+            )
+        )
+    x_rows[f] = frames_ref[f]
+
+    capf = cap_ref[...].astype(jnp.float32)
+    cnorm = jnp.sqrt(jnp.sum(capf * capf, axis=1, keepdims=True) + 1e-06)
+    vunit = capf / cnorm
+    v_own = vunit.astype(jnp.bfloat16)
+    v32[c, f] = v_own.astype(jnp.float32)
+    for d in range(1, C):
+        go(remote(v32.at[c, f], v32.at[c, f], v1_send.at[d], v1_recv.at[d], (cpeer(d), f)))
+
+    for d in range(1, F):
+        source = fpeer(F - d)
+        remote(
+            x_rows.at[source], x_rows.at[source], fr_send.at[d], fr_recv.at[d], (c, source)
+        ).wait_recv()
+    xf = x_rows[...].reshape(ROWS, D).astype(jnp.float32)
+    xt[...] = xf.T.astype(jnp.bfloat16).reshape(C, RC, ROWS)
+    for d in range(1, C):
+        to = cpeer(d)
+        go(remote(xt.at[to], xu.at[c, f], x1_send.at[d], x1_recv.at[d], (to, f)))
+    xu[c, f] = xt[c]
+
+    edge = jnp.zeros((NB, D), jnp.float32)
+    before = jnp.concatenate([edge, xf[: ROWS - NB]], axis=0).astype(jnp.bfloat16)
+    after = jnp.concatenate([xf[NB:], edge], axis=0).astype(jnp.bfloat16)
+    w_copies[0].wait()
+    conv = jnp.dot(before, w_ref[0], preferred_element_type=jnp.float32)
+
+    for d in range(1, C):
+        source = cpeer(C - d)
+        slot = v32.at[source, f]
+        remote(slot, slot, v1_send.at[d], v1_recv.at[d], (source, f)).wait_recv()
+    for d in range(1, F):
+        slab = v32.at[:, f]
+        go(remote(slab, slab, v2_send.at[d], v2_recv.at[d], (c, fpeer(d))))
+
+    w_copies[1].wait()
+    conv = conv + jnp.dot(
+        x_rows[...].reshape(ROWS, D), w_ref[1], preferred_element_type=jnp.float32
+    )
+    w_copies[2].wait()
+    conv = conv + jnp.dot(after, w_ref[2], preferred_element_type=jnp.float32)
+
+    scale = math.sqrt(2.0 / math.pi)
+    square = conv * conv
+    tanh = jnp.tanh(scale * conv * (1.0 + 0.044715 * square))
+    cdf = 0.5 * (1.0 + tanh)
+    slope[...] = cdf + (0.5 * scale) * conv * (1.0 - tanh * tanh) * (1.0 + 0.134145 * square)
+    hidden = xf + conv * cdf
+    pooled = jnp.sum(hidden.reshape(T, NB, D), axis=0) * (1.0 / T)
+    pnorm = jnp.sqrt(jnp.sum(pooled * pooled, axis=1, keepdims=True) + 1e-06)
+    unit = pooled / pnorm
+    u_low = unit.astype(jnp.bfloat16)
+    pos_own = pos_ref[f]
+    u32[c, f, :, :D] = u_low.astype(jnp.float32)
+    u32[c, f, :, D:] = pos_own
+    for d in range(1, C):
+        go(remote(u32.at[c, f], u32.at[c, f], u1_send.at[d], u1_recv.at[d], (cpeer(d), f)))
+
+    for d in range(1, F):
+        slab = v32.at[:, fpeer(F - d)]
+        remote(slab, slab, v2_send.at[d], v2_recv.at[d], (c, fpeer(F - d))).wait_recv()
+    caps = C * F * NB
+    vb[...] = v32[...].reshape(caps, D).astype(jnp.bfloat16)
+    logits = 10.0 * nt_dot(u_low, vb[...]) - 10.0
+    ids = lax.broadcasted_iota(jnp.int32, (NB, caps), 1).astype(jnp.float32)
+    match = jnp.where(pos_own[:, :1] == ids, 1.0, 0.0)
+    coef = (10.0 * (1.0 / (1.0 + jnp.exp(-logits)) - match)).astype(jnp.bfloat16)
+    du = jnp.dot(coef, vb[...], preferred_element_type=jnp.float32)
+    dpooled = (du - unit * jnp.sum(unit * du, axis=1, keepdims=True)) / pnorm
+    step = dpooled * (1.0 / T)
+    dconv = (slope[...].reshape(T, NB, D) * step[None]).reshape(ROWS, D)
+    dt[...] = dconv.T.astype(jnp.bfloat16).reshape(F, CC, ROWS)
+    for d in range(1, F):
+        to = fpeer(d)
+        go(remote(dt.at[to], dbuf.at[c, f], da_send.at[d], da_recv.at[d], (c, to)))
+    dbuf[c, f] = dt[f]
+
+    ways = (right, left)
+
+    def block_at(way, hop):
+        return ring_to_clip(lax.rem(pos + (C - hop if way == 0 else hop), C), C)
+
+    def units_at(way, hop):
+        if hop < half:
+            return range(F)
+        return range(F // 2) if way == 0 else range(F // 2, F)
+
+    def forward(way, hop, q):
+        slot = dbuf.at[block_at(way, hop), fpeer(F - q)]
+        go(
+            remote(
+                slot,
+                slot,
+                ring_send.at[way, hop, q],
+                ring_recv.at[way, hop, q],
+                (ways[way], f),
+            )
+        )
+
+    def arrive(way, hop, q):
+        slot = dbuf.at[block_at(way, hop), fpeer(F - q)]
+        remote(
+            slot,
+            slot,
+            ring_send.at[way, hop - 1, q],
+            ring_recv.at[way, hop - 1, q],
+            (ways[way], f),
+        ).wait_recv()
+
+    def relay(hop):
+        for q in range(F):
+            for way in range(2):
+                if q in units_at(way, hop):
+                    arrive(way, hop, q)
+                    if hop < half and q in units_at(way, hop + 1):
+                        forward(way, hop, q)
+
+    def add_block(block, first=False):
+        rhs = jnp.concatenate([dbuf[block, i] for i in range(F)], axis=1)
+        term = nt_dot(x3[block], rhs)
+        if first:
+            acc[...] = term
+        else:
+            acc[...] += term
+
+    for q in range(F):
+        if q:
+            source = fpeer(F - q)
+            slot = dbuf.at[c, source]
+            remote(slot, slot, da_send.at[q], da_recv.at[q], (c, source)).wait_recv()
+        for way in range(2):
+            if q in units_at(way, 1):
+                forward(way, 0, q)
+
+    for d in range(1, C):
+        source = cpeer(C - d)
+        slot = xu.at[source, f]
+        remote(slot, slot, x1_send.at[d], x1_recv.at[d], (source, f)).wait_recv()
+    for d in range(1, F):
+        slab = xu.at[:, f]
+        go(remote(slab, slab, x2_send.at[d], x2_recv.at[d], (c, fpeer(d))))
+    for d in range(1, C):
+        source = cpeer(C - d)
+        slot = u32.at[source, f]
+        remote(slot, slot, u1_send.at[d], u1_recv.at[d], (source, f)).wait_recv()
+    for d in range(1, F):
+        slab = u32.at[:, f]
+        go(remote(slab, slab, u2_send.at[d], u2_recv.at[d], (c, fpeer(d))))
+
+    relay(1)
+    for d in range(1, F):
+        slab = xu.at[:, fpeer(F - d)]
+        remote(slab, slab, x2_send.at[d], x2_recv.at[d], (c, fpeer(F - d))).wait_recv()
+    row = lax.broadcasted_iota(jnp.int32, (ROWS, ROWS), 0)
+    col = lax.broadcasted_iota(jnp.int32, (ROWS, ROWS), 1)
+    later = jnp.where(row == col - NB, 1.0, 0.0)
+    earlier = jnp.where(row == col + NB, 1.0, 0.0)
+    moves = jnp.concatenate([later, earlier], axis=1).astype(jnp.bfloat16)
+
+    def shift(block, carry):
+        units = xu[block]
+        moved = jnp.dot(
+            units.reshape(F * RC, ROWS), moves, preferred_element_type=jnp.float32
+        ).astype(jnp.bfloat16)
+        for i in range(F):
+            lanes = slice(i * ROWS, (i + 1) * ROWS)
+            rows = slice(i * RC, (i + 1) * RC)
+            x3[block, 0:RC, lanes] = moved[rows, :ROWS]
+            x3[block, RC : 2 * RC, lanes] = units[i]
+            x3[block, 2 * RC :, lanes] = moved[rows, ROWS:]
+        return carry
+
+    lax.fori_loop(0, C, shift, 0)
+    add_block(c, first=True)
+
+    relay(2)
+    add_block(block_at(0, 1))
+    add_block(block_at(1, 1))
+
+    for d in range(1, F):
+        slab = u32.at[:, fpeer(F - d)]
+        remote(slab, slab, u2_send.at[d], u2_recv.at[d], (c, fpeer(F - d))).wait_recv()
+    ub[...] = u32[:, :, :, :D].reshape(caps, D).astype(jnp.bfloat16)
+    pos_all = u32[:, :, :, D:].reshape(caps, u32.shape[3] - D)
+    pos_row = pos_all.T[:1]
+    first_id = (c * F + f) * NB
+    own_ids = (first_id + lax.broadcasted_iota(jnp.int32, (NB, caps), 0)).astype(jnp.float32)
+    match_own = jnp.where(pos_row == own_ids, 1.0, 0.0)
+    logits_own = 10.0 * nt_dot(v_own, ub[...]) - 10.0
+    coef_own = (10.0 * (1.0 / (1.0 + jnp.exp(-logits_own)) - match_own)).astype(jnp.bfloat16)
+    dv = jnp.dot(coef_own, ub[...], preferred_element_type=jnp.float32)
+    gc_ref[...] = (dv - vunit * jnp.sum(vunit * dv, axis=1, keepdims=True)) / cnorm
+
+    relay(3)
+    add_block(block_at(0, 2))
+    add_block(block_at(1, 2))
+
+    every = 10.0 * nt_dot(ub[...], vb[...]) - 10.0
+    all_ids = lax.broadcasted_iota(jnp.int32, (caps, caps), 1).astype(jnp.float32)
+    signed = jnp.where(pos_all[:, :1] == all_ids, -every, every)
+    soft = jnp.maximum(signed, 0.0) + jnp.log1p(jnp.exp(-jnp.abs(signed)))
+    total = jnp.sum(jnp.sum(soft, axis=0, keepdims=True), axis=1, keepdims=True)
+    loss_ref[...] = jnp.broadcast_to(total * (1.0 / caps), loss_ref.shape)
+
+    add_block(block_at(0, 3))
+    add_block(block_at(1, 3))
+    relay(4)
+    add_block(block_at(0, 4))
+    gw_ref[...] = acc[...].reshape(3, RC, CC)
+    for copy in sends:
+        copy.wait_send()
+
+
+def fused(C, F, frames, conv_weight, captions, positive):
+    clip_dev, fr_dev, D = frames.shape
+    NB = clip_dev // F
+    ROWS = FRAMES * NB
+    RC, CC = D // C, D // F
+    half = C // 2
+    blocks = frames.reshape(F, NB, fr_dev, D).transpose(0, 2, 1, 3).reshape(F, fr_dev * NB, D)
+    ids = jnp.broadcast_to(positive.astype(jnp.float32).reshape(F, NB, 1), (F, NB, 128))
+    vmem = pl.BlockSpec(memory_space=pltpu.VMEM)
+    dma = pltpu.SemaphoreType.DMA
+    bf16, f32 = jnp.bfloat16, jnp.float32
+    caps = C * F * NB
+    loss, grad_weight, grad_captions = pl.pallas_call(
+        functools.partial(fused_kernel, C, F),
+        out_shape=(
+            jax.ShapeDtypeStruct((8, 128), f32),
+            jax.ShapeDtypeStruct((3, RC, CC), f32),
+            jax.ShapeDtypeStruct((NB, D), f32),
+        ),
+        in_specs=[vmem, pl.BlockSpec(memory_space=pl.ANY), vmem, vmem],
+        out_specs=(vmem, vmem, vmem),
+        scratch_shapes=[
+            pltpu.VMEM((3, D, D), bf16),
+            pltpu.VMEM((F, ROWS // F, D), bf16),
+            pltpu.VMEM((C, RC, ROWS), bf16),
+            pltpu.VMEM((C, F, RC, ROWS), bf16),
+            pltpu.VMEM((C, 3 * RC, F * ROWS), bf16),
+            pltpu.VMEM((C, F, NB, D), f32),
+            pltpu.VMEM((caps, D), bf16),
+            pltpu.VMEM((C, F, NB, D + 128), f32),
+            pltpu.VMEM((caps, D), bf16),
+            pltpu.VMEM((ROWS, D), f32),
+            pltpu.VMEM((F, CC, ROWS), bf16),
+            pltpu.VMEM((C, F, CC, ROWS), bf16),
+            pltpu.VMEM((3 * RC, CC), f32),
+            dma((3,)),
+            dma((F,)),
+            dma((F,)),
+            dma((C,)),
+            dma((C,)),
+            dma((F,)),
+            dma((F,)),
+            dma((C,)),
+            dma((C,)),
+            dma((F,)),
+            dma((F,)),
+            dma((C,)),
+            dma((C,)),
+            dma((F,)),
+            dma((F,)),
+            dma((F,)),
+            dma((F,)),
+            dma((2, half, F)),
+            dma((2, half, F)),
+        ],
+        compiler_params=pltpu.CompilerParams(
+            collective_id=0, has_side_effects=True, vmem_limit_bytes=52 * 1024 * 1024
+        ),
+        cost_estimate=pl.CostEstimate(
+            flops=4 * 3 * ROWS * D * D, bytes_accessed=8 * D * D, transcendentals=ROWS * D
+        ),
+    )(blocks, conv_weight, captions, ids)
+    return loss[0, 0], grad_weight, grad_captions
+
+
+def fits(C, F, frames, captions):
+    clip_dev, fr_dev, D = frames.shape
+    clips = clip_dev // F
+    return (
+        C == 8
+        and F == 4
+        and clips == 8
+        and clip_dev % F == 0
+        and captions.shape[0] == clips
+        and fr_dev * F == FRAMES
+        and D % (16 * C) == 0
+        and D % 128 == 0
+    )
+
+
+def on_device(frames, conv_weight, captions, positive):
+    C, F = lax.axis_size("clip"), lax.axis_size("frame")
+    if fits(C, F, frames, captions):
+        return fused(C, F, frames, conv_weight, captions, positive)
+    return plain(frames, conv_weight, captions, positive)
+
+
 def solution(mesh):
     placed = (P("clip", "frame", None), P(), P(("clip", "frame"), None), P("clip"))
     return jax.shard_map(

time: 298 us -> 74.7 us (0.25)
  the two profiles are of different devices: /device:TPU:0 before, /device:TPU:1 now
where the time goes in v1:
time: 74.7 us; the launch traced here: 74.5 us
  Pallas kernels  69.4 us (93%)
  local copies, waits for them, and re-layouts  3.84 us (5%)
    pallas_call x1, Pallas kernels, fused(): pl.pallas_call(functools.partial(fused_kernel, C, F), out_shape=(jax.Shap...  69.4 us
    unnamed x4, local copies, waits for them, and re-layouts  2.17 us

profile of v1, /device:TPU:1, one launch (start us, length us, event | category | flops | bytes accessed | tf_op | source)
XLA Modules:
  0.0 74.5 jit_solution(9240825616976602756)
XLA Ops:
  0.6 0.7 convert_element_type.3
  1.3 0.1 broadcast_in_dim.7
  1.4 0.1 broadcast_in_dim.8.pos_ref
  1.4 1.0 %copy.9 = bf16[4,8,4,1152]{3,1,2,0:T(8,128)(2,1)S(1)} copy(bf16[4,8,4,1152]{3,2,1,0:T(4,128)(2,1)} %bitcast.8) | data formatting | bytes 589824 | tf_op jit(solution)/shard_map/reshape | solution.py:429
  2.4 0.0 copy-start
  2.5 0.7 copy-done
  3.2 69.4 %shard_map.67 = (f32[8,128]{1,0:T(8,128)S(1)}, f32[3,144,288]{2,1,0:T(8,128)S(1)}, f32[8,1152]{1,0:T(8,128)S(1)}) custom-call(bf16[4,32,1152]{2,1,0:T(8,128)(2,1)S(1)} %bitcast.7, bf16[3,1152,1152]{2,1,0:T(8,128)(2,1)} %w_hbm.1, bf16[8,1152]{1,0:T(8,128)(2,1)S(1)} %copy-done, f32[4,8,128]{2,1,0:T(8,128)S(1)} %broadcast_in_dim.8.pos_ref), custom_call_target="tpu_custom_call" | custom-call | flops 2038431744 | bytes 10616832 | tf_op jit(solution)/shard_map/pallas_call | solution.py:435
  72.5 0.5 slice.3
  73.1 0.8 %copy.12 = f32[3,144,288]{2,1,0:T(8,128)} copy(f32[3,144,288]{2,1,0:T(8,128)S(1)} %get-tuple-element.13) | data formatting | bytes 995328
  73.9 0.6 copy.13
Async XLA Ops:
  2.4 0.7 copy-start

commit v2 on v1

--- a/solution.py
+++ b/solution.py
@@ -115,6 +115,21 @@
     return 2 * r + high * (2 * count - 1 - 4 * r)
 
 
+def pack(rows, extra):
+    cut = (rows.shape[1] + extra.shape[1]) // 2
+    bottom = jnp.concatenate([rows[:, cut:], extra], axis=1)
+    return jnp.concatenate([rows[:, :cut], bottom], axis=0).astype(jnp.bfloat16)
+
+
+def unpack(units, width):
+    C, F, tall, cut = units.shape
+    flat = units.reshape(C * F, tall, cut).astype(jnp.float32)
+    top = flat[:, : tall // 2].reshape(C * F * tall // 2, cut)
+    bottom = flat[:, tall // 2 :].reshape(C * F * tall // 2, cut)
+    rows = jnp.concatenate([top, bottom[:, : width - cut]], axis=1)
+    return rows.astype(jnp.bfloat16), bottom[:, width - cut :]
+
+
 def fused_kernel(
     C,
     F,
@@ -122,6 +137,7 @@
     w_hbm,
     cap_ref,
     pos_ref,
+    split_ref,
     loss_ref,
     gw_ref,
     gc_ref,
@@ -130,9 +146,9 @@
     xt,
     xu,
     x3,
-    v32,
+    vu,
     vb,
-    u32,
+    uu,
     ub,
     slope,
     dt,
@@ -196,6 +212,31 @@
         copy.start()
         sends.append(copy)
 
+    across = lax.rem(f + F // 2, F)
+    beside = f + 1 - 2 * lax.rem(f, 2)
+    diagonal = lax.rem(beside + F // 2, F)
+
+    def spread(array, send_sem, recv_sem):
+        slab = array.at[:, f]
+        go(remote(slab, slab, send_sem.at[0], recv_sem.at[0], (c, across)))
+        go(remote(slab, slab, send_sem.at[1], recv_sem.at[1], (c, beside)))
+
+    def spread_on(array, send_sem, recv_sem):
+        slab = array.at[:, across]
+        remote(slab, slab, send_sem.at[0], recv_sem.at[0], (c, across)).wait_recv()
+        go(remote(slab, slab, send_sem.at[2], recv_sem.at[2], (c, beside)))
+
+    def spread_end(array, send_sem, recv_sem):
+        for i, source in ((1, beside), (2, diagonal)):
+            slab = array.at[:, source]
+            remote(slab, slab, send_sem.at[i], recv_sem.at[i], (c, beside)).wait_recv()
+
+    def clip_arrive(array, send_sem, recv_sem):
+        for d in range(1, C):
+            source = cpeer(C - d)
+            slot = array.at[source, f]
+            remote(slot, slot, send_sem.at[d], recv_sem.at[d], (source, f)).wait_recv()
+
     for d in range(1, F):
         go(
             remote(
@@ -212,9 +253,9 @@
     cnorm = jnp.sqrt(jnp.sum(capf * capf, axis=1, keepdims=True) + 1e-06)
     vunit = capf / cnorm
     v_own = vunit.astype(jnp.bfloat16)
-    v32[c, f] = v_own.astype(jnp.float32)
+    vu[c, f] = pack(v_own.astype(jnp.float32), jnp.zeros((NB, 128), jnp.float32))
     for d in range(1, C):
-        go(remote(v32.at[c, f], v32.at[c, f], v1_send.at[d], v1_recv.at[d], (cpeer(d), f)))
+        go(remote(vu.at[c, f], vu.at[c, f], v1_send.at[d], v1_recv.at[d], (cpeer(d), f)))
 
     for d in range(1, F):
         source = fpeer(F - d)
@@ -234,20 +275,19 @@
     w_copies[0].wait()
     conv = jnp.dot(before, w_ref[0], preferred_element_type=jnp.float32)
 
-    for d in range(1, C):
-        source = cpeer(C - d)
-        slot = v32.at[source, f]
-        remote(slot, slot, v1_send.at[d], v1_recv.at[d], (source, f)).wait_recv()
-    for d in range(1, F):
-        slab = v32.at[:, f]
-        go(remote(slab, slab, v2_send.at[d], v2_recv.at[d], (c, fpeer(d))))
+    clip_arrive(vu, v1_send, v1_recv)
+    spread(vu, v2_send, v2_recv)
 
     w_copies[1].wait()
     conv = conv + jnp.dot(
         x_rows[...].reshape(ROWS, D), w_ref[1], preferred_element_type=jnp.float32
     )
+    clip_arrive(xu, x1_send, x1_recv)
+    spread(xu, x2_send, x2_recv)
     w_copies[2].wait()
     conv = conv + jnp.dot(after, w_ref[2], preferred_element_type=jnp.float32)
+
+    spread_on(vu, v2_send, v2_recv)
 
     scale = math.sqrt(2.0 / math.pi)
     square = conv * conv
@@ -260,16 +300,13 @@
     unit = pooled / pnorm
     u_low = unit.astype(jnp.bfloat16)
     pos_own = pos_ref[f]
-    u32[c, f, :, :D] = u_low.astype(jnp.float32)
-    u32[c, f, :, D:] = pos_own
+    uu[c, f] = pack(u_low.astype(jnp.float32), split_ref[f])
     for d in range(1, C):
-        go(remote(u32.at[c, f], u32.at[c, f], u1_send.at[d], u1_recv.at[d], (cpeer(d), f)))
-
-    for d in range(1, F):
-        slab = v32.at[:, fpeer(F - d)]
-        remote(slab, slab, v2_send.at[d], v2_recv.at[d], (c, fpeer(F - d))).wait_recv()
+        go(remote(uu.at[c, f], uu.at[c, f], u1_send.at[d], u1_recv.at[d], (cpeer(d), f)))
+
+    spread_end(vu, v2_send, v2_recv)
     caps = C * F * NB
-    vb[...] = v32[...].reshape(caps, D).astype(jnp.bfloat16)
+    vb[...] = unpack(vu[...], D)[0]
     logits = 10.0 * nt_dot(u_low, vb[...]) - 10.0
     ids = lax.broadcasted_iota(jnp.int32, (NB, caps), 1).astype(jnp.float32)
     match = jnp.where(pos_own[:, :1] == ids, 1.0, 0.0)
@@ -341,25 +378,8 @@
             if q in units_at(way, 1):
                 forward(way, 0, q)
 
-    for d in range(1, C):
-        source = cpeer(C - d)
-        slot = xu.at[source, f]
-        remote(slot, slot, x1_send.at[d], x1_recv.at[d], (source, f)).wait_recv()
-    for d in range(1, F):
-        slab = xu.at[:, f]
-        go(remote(slab, slab, x2_send.at[d], x2_recv.at[d], (c, fpeer(d))))
-    for d in range(1, C):
-        source = cpeer(C - d)
-        slot = u32.at[source, f]
-        remote(slot, slot, u1_send.at[d], u1_recv.at[d], (source, f)).wait_recv()
-    for d in range(1, F):
-        slab = u32.at[:, f]
-        go(remote(slab, slab, u2_send.at[d], u2_recv.at[d], (c, fpeer(d))))
-
-    relay(1)
-    for d in range(1, F):
-        slab = xu.at[:, fpeer(F - d)]
-        remote(slab, slab, x2_send.at[d], x2_recv.at[d], (c, fpeer(F - d))).wait_recv()
+    spread_on(xu, x2_send, x2_recv)
+    spread_end(xu, x2_send, x2_recv)
     row = lax.broadcasted_iota(jnp.int32, (ROWS, ROWS), 0)
     col = lax.broadcasted_iota(jnp.int32, (ROWS, ROWS), 1)
     later = jnp.where(row == col - NB, 1.0, 0.0)
@@ -382,16 +402,25 @@
     lax.fori_loop(0, C, shift, 0)
     add_block(c, first=True)
 
-    relay(2)
+    relay(1)
+    clip_arrive(uu, u1_send, u1_recv)
+    spread(uu, u2_send, u2_recv)
     add_block(block_at(0, 1))
     add_block(block_at(1, 1))
 
-    for d in range(1, F):
-        slab = u32.at[:, fpeer(F - d)]
-        remote(slab, slab, u2_send.at[d], u2_recv.at[d], (c, fpeer(F - d))).wait_recv()
-    ub[...] = u32[:, :, :, :D].reshape(caps, D).astype(jnp.bfloat16)
-    pos_all = u32[:, :, :, D:].reshape(caps, u32.shape[3] - D)
-    pos_row = pos_all.T[:1]
+    relay(2)
+    spread_on(uu, u2_send, u2_recv)
+    add_block(block_at(0, 2))
+    add_block(block_at(1, 2))
+
+    relay(3)
+
+    spread_end(uu, u2_send, u2_recv)
+    u_all, halves = unpack(uu[...], D)
+    ub[...] = u_all
+    pos_all = 128.0 * halves[:, :1] + halves[:, 64:65]
+    turned = halves.T
+    pos_row = 128.0 * turned[:1] + turned[64:65]
     first_id = (c * F + f) * NB
     own_ids = (first_id + lax.broadcasted_iota(jnp.int32, (NB, caps), 0)).astype(jnp.float32)
     match_own = jnp.where(pos_row == own_ids, 1.0, 0.0)
@@ -400,13 +429,9 @@
     dv = jnp.dot(coef_own, ub[...], preferred_element_type=jnp.float32)
     gc_ref[...] = (dv - vunit * jnp.sum(vunit * dv, axis=1, keepdims=True)) / cnorm
 
-    relay(3)
-    add_block(block_at(0, 2))
-    add_block(block_at(1, 2))
-
     every = 10.0 * nt_dot(ub[...], vb[...]) - 10.0
     all_ids = lax.broadcasted_iota(jnp.int32, (caps, caps), 1).astype(jnp.float32)
-    signed = jnp.where(pos_all[:, :1] == all_ids, -every, every)
+    signed = jnp.where(pos_all == all_ids, -every, every)
     soft = jnp.maximum(signed, 0.0) + jnp.log1p(jnp.exp(-jnp.abs(signed)))
     total = jnp.sum(jnp.sum(soft, axis=0, keepdims=True), axis=1, keepdims=True)
     loss_ref[...] = jnp.broadcast_to(total * (1.0 / caps), loss_ref.shape)
@@ -427,7 +452,9 @@
     RC, CC = D // C, D // F
     half = C // 2
     blocks = frames.reshape(F, NB, fr_dev, D).transpose(0, 2, 1, 3).reshape(F, fr_dev * NB, D)
-    ids = jnp.broadcast_to(positive.astype(jnp.float32).reshape(F, NB, 1), (F, NB, 128))
+    ids = jnp.broadcast_to(positive.reshape(F, NB, 1), (F, NB, 128))
+    split = jnp.where(jnp.arange(128) < 64, ids // 128, ids % 128).astype(jnp.float32)
+    ids = ids.astype(jnp.float32)
     vmem = pl.BlockSpec(memory_space=pltpu.VMEM)
     dma = pltpu.SemaphoreType.DMA
     bf16, f32 = jnp.bfloat16, jnp.float32
@@ -439,7 +466,7 @@
             jax.ShapeDtypeStruct((3, RC, CC), f32),
             jax.ShapeDtypeStruct((NB, D), f32),
         ),
-        in_specs=[vmem, pl.BlockSpec(memory_space=pl.ANY), vmem, vmem],
+        in_specs=[vmem, pl.BlockSpec(memory_space=pl.ANY), vmem, vmem, vmem],
         out_specs=(vmem, vmem, vmem),
         scratch_shapes=[
             pltpu.VMEM((3, D, D), bf16),
@@ -447,9 +474,9 @@
             pltpu.VMEM((C, RC, ROWS), bf16),
             pltpu.VMEM((C, F, RC, ROWS), bf16),
             pltpu.VMEM((C, 3 * RC, F * ROWS), bf16),
-            pltpu.VMEM((C, F, NB, D), f32),
+            pltpu.VMEM((C, F, 2 * NB, (D + 128) // 2), bf16),
             pltpu.VMEM((caps, D), bf16),
-            pltpu.VMEM((C, F, NB, D + 128), f32),
+            pltpu.VMEM((C, F, 2 * NB, (D + 128) // 2), bf16),
             pltpu.VMEM((caps, D), bf16),
             pltpu.VMEM((ROWS, D), f32),
             pltpu.VMEM((F, CC, ROWS), bf16),
@@ -481,7 +508,7 @@
         cost_estimate=pl.CostEstimate(
             flops=4 * 3 * ROWS * D * D, bytes_accessed=8 * D * D, transcendentals=ROWS * D
         ),
-    )(blocks, conv_weight, captions, ids)
+    )(blocks, conv_weight, captions, ids, split)
     return loss[0, 0], grad_weight, grad_captions
 
 

time: 74.7 us -> 57.6 us (0.77)
  the two profiles are of different devices: /device:TPU:1 before, /device:TPU:0 now
where the time goes in v2:
time: 57.6 us; the launch traced here: 56.8 us
  Pallas kernels  51.5 us (89%)
  local copies, waits for them, and re-layouts  4.49 us (8%)
  between operations  0.67 us (1%)
    pallas_call x1, Pallas kernels, fused(): pl.pallas_call(functools.partial(fused_kernel, C, F), out_shape=(jax.Shap...  51.5 us
    unnamed x4, local copies, waits for them, and re-layouts  2.17 us

profile of v2, /device:TPU:0, one launch (start us, length us, event | category | flops | bytes accessed | tf_op | source)
XLA Modules:
  0.0 56.8 jit_solution(12403562534291460055)
XLA Ops:
  0.6 0.7 %broadcast_in_dim.23 = s32[4,8]{1,0:T(4,128)S(1)} reshape(s32[32]{0:T(128)} %param.7) | data formatting | bytes 256 | tf_op jit(solution)/shard_map/broadcast_in_dim | solution.py:455
  1.4 0.1 select_convert_fusion.split_ref
  1.5 0.1 broadcast_in_dim.24.pos_ref
  1.6 1.0 %copy.9 = bf16[4,8,4,1152]{3,1,2,0:T(8,128)(2,1)S(1)} copy(bf16[4,8,4,1152]{3,2,1,0:T(4,128)(2,1)} %bitcast.8) | data formatting | bytes 589824 | tf_op jit(solution)/shard_map/reshape | solution.py:454
  2.6 0.0 copy-start
  2.6 0.7 %copy-done = bf16[8,1152]{1,0:T(8,128)(2,1)S(1)} copy-done((bf16[8,1152]{1,0:T(8,128)(2,1)S(1)}, bf16[8,1152]{1,0:T(8,128)(2,1)}, u32[]{:S(2)}) %copy-start) | copy-done | bytes 18456
  3.3 51.5 %shard_map.67 = (f32[8,128]{1,0:T(8,128)S(1)}, f32[3,144,288]{2,1,0:T(8,128)S(1)}, f32[8,1152]{1,0:T(8,128)S(1)}) custom-call(bf16[4,32,1152]{2,1,0:T(8,128)(2,1)S(1)} %bitcast.7, bf16[3,1152,1152]{2,1,0:T(8,128)(2,1)} %w_hbm.1, bf16[8,1152]{1,0:T(8,128)(2,1)S(1)} %copy-done, f32[4,8,128]{2,1,0:T(8,128)S(1)} %broadcast_in_dim.24.pos_ref, ...), custom_call_target="tpu_custom_call" | custom-call | flops 2038431744 | bytes 10616832 | tf_op jit(solution)/shard_map/pallas_call | solution.py:462
  54.8 0.5 slice.3
  55.4 0.8 %copy.12 = f32[3,144,288]{2,1,0:T(8,128)} copy(f32[3,144,288]{2,1,0:T(8,128)S(1)} %get-tuple-element.20) | data formatting | bytes 995328
  56.2 0.6 %copy.13 = f32[8,1152]{1,0:T(8,128)} copy(f32[8,1152]{1,0:T(8,128)S(1)} %get-tuple-element.21) | data formatting | bytes 73728
  (3 shorter events, 0.0 us)
Async XLA Ops:
  2.6 0.7 %copy-start = (bf16[8,1152]{1,0:T(8,128)(2,1)S(1)}, bf16[8,1152]{1,0:T(8,128)(2,1)}, u32[]{:S(2)}) copy-start(bf16[8,1152]{1,0:T(8,128)(2,1)} %cap_ref.1) | copy-start | bytes 55300

commit v3 on v2

--- a/solution.py
+++ b/solution.py
@@ -135,12 +135,13 @@
     F,
     frames_ref,
     w_hbm,
-    cap_ref,
-    pos_ref,
-    split_ref,
+    cap_hbm,
+    pos_hbm,
     loss_ref,
     gw_ref,
     gc_ref,
+    cap_ref,
+    pos_ref,
     w_ref,
     x_rows,
     xt,
@@ -154,6 +155,8 @@
     dt,
     dbuf,
     acc,
+    cap_sem,
+    pos_sem,
     w_sem,
     fr_send,
     fr_recv,
@@ -189,6 +192,10 @@
     right = ring_to_clip(lax.rem(pos + 1, C), C)
     left = ring_to_clip(lax.rem(pos + C - 1, C), C)
 
+    cap_copy = pltpu.make_async_copy(cap_hbm, cap_ref, cap_sem)
+    cap_copy.start()
+    pos_copy = pltpu.make_async_copy(pos_hbm, pos_ref, pos_sem)
+    pos_copy.start()
     w_copies = [pltpu.make_async_copy(w_hbm.at[k], w_ref.at[k], w_sem.at[k]) for k in range(3)]
     for copy in w_copies:
         copy.start()
@@ -249,6 +256,8 @@
         )
     x_rows[f] = frames_ref[f]
 
+    cap_copy.wait()
+    pos_copy.wait()
     capf = cap_ref[...].astype(jnp.float32)
     cnorm = jnp.sqrt(jnp.sum(capf * capf, axis=1, keepdims=True) + 1e-06)
     vunit = capf / cnorm
@@ -263,18 +272,17 @@
             x_rows.at[source], x_rows.at[source], fr_send.at[d], fr_recv.at[d], (c, source)
         ).wait_recv()
     xf = x_rows[...].reshape(ROWS, D).astype(jnp.float32)
+    edge = jnp.zeros((NB, D), jnp.float32)
+    before = jnp.concatenate([edge, xf[: ROWS - NB]], axis=0).astype(jnp.bfloat16)
+    after = jnp.concatenate([xf[NB:], edge], axis=0).astype(jnp.bfloat16)
+    w_copies[0].wait()
+    conv = jnp.dot(before, w_ref[0], preferred_element_type=jnp.float32)
     xt[...] = xf.T.astype(jnp.bfloat16).reshape(C, RC, ROWS)
     for d in range(1, C):
         to = cpeer(d)
         go(remote(xt.at[to], xu.at[c, f], x1_send.at[d], x1_recv.at[d], (to, f)))
     xu[c, f] = xt[c]
 
-    edge = jnp.zeros((NB, D), jnp.float32)
-    before = jnp.concatenate([edge, xf[: ROWS - NB]], axis=0).astype(jnp.bfloat16)
-    after = jnp.concatenate([xf[NB:], edge], axis=0).astype(jnp.bfloat16)
-    w_copies[0].wait()
-    conv = jnp.dot(before, w_ref[0], preferred_element_type=jnp.float32)
-
     clip_arrive(vu, v1_send, v1_recv)
     spread(vu, v2_send, v2_recv)
 
@@ -282,8 +290,6 @@
     conv = conv + jnp.dot(
         x_rows[...].reshape(ROWS, D), w_ref[1], preferred_element_type=jnp.float32
     )
-    clip_arrive(xu, x1_send, x1_recv)
-    spread(xu, x2_send, x2_recv)
     w_copies[2].wait()
     conv = conv + jnp.dot(after, w_ref[2], preferred_element_type=jnp.float32)
 
@@ -299,17 +305,26 @@
     pnorm = jnp.sqrt(jnp.sum(pooled * pooled, axis=1, keepdims=True) + 1e-06)
     unit = pooled / pnorm
     u_low = unit.astype(jnp.bfloat16)
-    pos_own = pos_ref[f]
-    uu[c, f] = pack(u_low.astype(jnp.float32), split_ref[f])
+    lanes = lax.broadcasted_iota(jnp.int32, (NB, F * NB), 1)
+    mine = lanes == f * NB + lax.broadcasted_iota(jnp.int32, (NB, F * NB), 0)
+    every_pos = jnp.broadcast_to(pos_ref[...].astype(jnp.float32), (NB, F * NB))
+    pos_own = jnp.sum(jnp.where(mine, every_pos, 0.0), axis=1, keepdims=True)
+    high = jnp.floor(pos_own * (1.0 / 128.0))
+    lane = lax.broadcasted_iota(jnp.int32, (NB, 128), 1)
+    split = jnp.where(lane < 64, high, pos_own - 128.0 * high)
+    uu[c, f] = pack(u_low.astype(jnp.float32), split)
     for d in range(1, C):
         go(remote(uu.at[c, f], uu.at[c, f], u1_send.at[d], u1_recv.at[d], (cpeer(d), f)))
+
+    clip_arrive(xu, x1_send, x1_recv)
+    spread(xu, x2_send, x2_recv)
 
     spread_end(vu, v2_send, v2_recv)
     caps = C * F * NB
     vb[...] = unpack(vu[...], D)[0]
     logits = 10.0 * nt_dot(u_low, vb[...]) - 10.0
     ids = lax.broadcasted_iota(jnp.int32, (NB, caps), 1).astype(jnp.float32)
-    match = jnp.where(pos_own[:, :1] == ids, 1.0, 0.0)
+    match = jnp.where(pos_own == ids, 1.0, 0.0)
     coef = (10.0 * (1.0 / (1.0 + jnp.exp(-logits)) - match)).astype(jnp.bfloat16)
     du = jnp.dot(coef, vb[...], preferred_element_type=jnp.float32)
     dpooled = (du - unit * jnp.sum(unit * du, axis=1, keepdims=True)) / pnorm
@@ -353,21 +368,23 @@
             (ways[way], f),
         ).wait_recv()
 
-    def relay(hop):
-        for q in range(F):
+    def relay(hop, *which):
+        for q in which:
             for way in range(2):
                 if q in units_at(way, hop):
                     arrive(way, hop, q)
                     if hop < half and q in units_at(way, hop + 1):
                         forward(way, hop, q)
 
+    def block_term(block):
+        rhs = jnp.concatenate([dbuf[block, i] for i in range(F)], axis=1)
+        return nt_dot(x3[block], rhs)
+
     def add_block(block, first=False):
-        rhs = jnp.concatenate([dbuf[block, i] for i in range(F)], axis=1)
-        term = nt_dot(x3[block], rhs)
         if first:
-            acc[...] = term
+            acc[...] = block_term(block)
         else:
-            acc[...] += term
+            acc[...] += block_term(block)
 
     for q in range(F):
         if q:
@@ -378,6 +395,7 @@
             if q in units_at(way, 1):
                 forward(way, 0, q)
 
+    relay(1, 0)
     spread_on(xu, x2_send, x2_recv)
     spread_end(xu, x2_send, x2_recv)
     row = lax.broadcasted_iota(jnp.int32, (ROWS, ROWS), 0)
@@ -399,22 +417,29 @@
             x3[block, 2 * RC :, lanes] = moved[rows, ROWS:]
         return carry
 
-    lax.fori_loop(0, C, shift, 0)
-    add_block(c, first=True)
-
-    relay(1)
+    quarter = C // 4
+    lax.fori_loop(0, quarter, shift, 0)
+    relay(1, 1)
+    lax.fori_loop(quarter, 2 * quarter, shift, 0)
+    relay(1, 2)
+    lax.fori_loop(2 * quarter, 3 * quarter, shift, 0)
+    relay(1, 3)
     clip_arrive(uu, u1_send, u1_recv)
     spread(uu, u2_send, u2_recv)
+    lax.fori_loop(3 * quarter, C, shift, 0)
+    relay(2, 0)
+    add_block(c, first=True)
+    relay(2, 1)
     add_block(block_at(0, 1))
+    relay(2, 2)
     add_block(block_at(1, 1))
-
-    relay(2)
+    relay(2, 3)
     spread_on(uu, u2_send, u2_recv)
+    relay(3, 0)
     add_block(block_at(0, 2))
+    relay(3, 1)
     add_block(block_at(1, 2))
-
-    relay(3)
-
+    relay(3, 2)
     spread_end(uu, u2_send, u2_recv)
     u_all, halves = unpack(uu[...], D)
     ub[...] = u_all
@@ -429,6 +454,7 @@
     dv = jnp.dot(coef_own, ub[...], preferred_element_type=jnp.float32)
     gc_ref[...] = (dv - vunit * jnp.sum(vunit * dv, axis=1, keepdims=True)) / cnorm
 
+    relay(3, 3)
     every = 10.0 * nt_dot(ub[...], vb[...]) - 10.0
     all_ids = lax.broadcasted_iota(jnp.int32, (caps, caps), 1).astype(jnp.float32)
     signed = jnp.where(pos_all == all_ids, -every, every)
@@ -438,9 +464,8 @@
 
     add_block(block_at(0, 3))
     add_block(block_at(1, 3))
-    relay(4)
-    add_block(block_at(0, 4))
-    gw_ref[...] = acc[...].reshape(3, RC, CC)
+    relay(4, *range(F))
+    gw_ref[...] = (acc[...] + block_term(block_at(0, 4))).reshape(3, RC, CC)
     for copy in sends:
         copy.wait_send()
 
@@ -452,10 +477,8 @@
     RC, CC = D // C, D // F
     half = C // 2
     blocks = frames.reshape(F, NB, fr_dev, D).transpose(0, 2, 1, 3).reshape(F, fr_dev * NB, D)
-    ids = jnp.broadcast_to(positive.reshape(F, NB, 1), (F, NB, 128))
-    split = jnp.where(jnp.arange(128) < 64, ids // 128, ids % 128).astype(jnp.float32)
-    ids = ids.astype(jnp.float32)
     vmem = pl.BlockSpec(memory_space=pltpu.VMEM)
+    hbm = pl.BlockSpec(memory_space=pltpu.HBM)
     dma = pltpu.SemaphoreType.DMA
     bf16, f32 = jnp.bfloat16, jnp.float32
     caps = C * F * NB
@@ -466,9 +489,11 @@
             jax.ShapeDtypeStruct((3, RC, CC), f32),
             jax.ShapeDtypeStruct((NB, D), f32),
         ),
-        in_specs=[vmem, pl.BlockSpec(memory_space=pl.ANY), vmem, vmem, vmem],
+        in_specs=[vmem, hbm, hbm, hbm],
         out_specs=(vmem, vmem, vmem),
         scratch_shapes=[
+            pltpu.VMEM((NB, D), bf16),
+            pltpu.VMEM((1, clip_dev), jnp.int32),
             pltpu.VMEM((3, D, D), bf16),
             pltpu.VMEM((F, ROWS // F, D), bf16),
             pltpu.VMEM((C, RC, ROWS), bf16),
@@ -482,6 +507,8 @@
             pltpu.VMEM((F, CC, ROWS), bf16),
             pltpu.VMEM((C, F, CC, ROWS), bf16),
             pltpu.VMEM((3 * RC, CC), f32),
+            dma,
+            dma,
             dma((3,)),
             dma((F,)),
             dma((F,)),
@@ -508,7 +535,7 @@
         cost_estimate=pl.CostEstimate(
             flops=4 * 3 * ROWS * D * D, bytes_accessed=8 * D * D, transcendentals=ROWS * D
         ),
-    )(blocks, conv_weight, captions, ids, split)
+    )(blocks, conv_weight, captions, positive.reshape(1, clip_dev))
     return loss[0, 0], grad_weight, grad_captions
 
 

time: 57.6 us -> 57.8 us (level)
  Pallas kernels: 51.5 us -> 52.6 us
    pallas_call x1, Pallas kernels: 51.5 us -> 52.6 us  [fused(): pl.pallas_call(functools.partial(fused_kernel, C, F), out_shape=(jax.Shap...]
    broadcast_in_dim x2 -> x0, local copies, waits for them, and re-layouts: 0.81 us -> none  [fused(): ids = jnp.broadcast_to(positive.reshape(F, NB, 1), (F, NB, 128))]
    unnamed x4 -> x6, local copies, waits for them, and re-layouts: 2.17 us -> 2.83 us
where the time goes in v3:
time: 57.8 us; the launch traced here: 57.6 us
  Pallas kernels  52.6 us (91%)
  local copies, waits for them, and re-layouts  4.33 us (7%)
  between operations  0.65 us (1%)
    pallas_call x1, Pallas kernels, fused(): pl.pallas_call(functools.partial(fused_kernel, C, F), out_shape=(jax.Shap...  52.6 us
    unnamed x6, local copies, waits for them, and re-layouts  2.83 us

profile of v3, /device:TPU:0, one launch (start us, length us, event | category | flops | bytes accessed | tf_op | source)
XLA Modules:
  0.0 57.6 jit_solution(7632572123610674102)
XLA Ops:
  0.6 1.0 %copy.9 = bf16[4,8,4,1152]{3,1,2,0:T(8,128)(2,1)S(1)} copy(bf16[4,8,4,1152]{3,2,1,0:T(4,128)(2,1)} %bitcast.10) | data formatting | bytes 589824 | tf_op jit(solution)/shard_map/reshape | solution.py:479
  1.6 0.0 copy-start
  1.6 0.7 %copy-done = bf16[8,1152]{1,0:T(8,128)(2,1)S(1)} copy-done((bf16[8,1152]{1,0:T(8,128)(2,1)S(1)}, bf16[8,1152]{1,0:T(8,128)(2,1)}, u32[]{:S(2)}) %copy-start) | copy-done | bytes 18456
  2.4 0.0 copy-start.1
  2.4 0.7 %copy-done.1 = s32[32]{0:T(128)S(1)} copy-done((s32[32]{0:T(128)S(1)}, s32[32]{0:T(128)}, u32[]{:S(2)}) %copy-start.1) | copy-done | bytes 152
  3.0 52.6 %shard_map.67 = (f32[8,128]{1,0:T(8,128)S(1)}, f32[3,144,288]{2,1,0:T(8,128)S(1)}, f32[8,1152]{1,0:T(8,128)S(1)}) custom-call(bf16[4,32,1152]{2,1,0:T(8,128)(2,1)S(1)} %bitcast.8, bf16[3,1152,1152]{2,1,0:T(8,128)(2,1)} %w_hbm.1, bf16[8,1152]{1,0:T(8,128)(2,1)S(1)} %copy-done, s32[1,32]{1,0:T(1,128)S(1)} %bitcast.9), custom_call_target="tpu_custom_call" | custom-call | flops 2038431744 | bytes 10616832 | tf_op jit(solution)/shard_map/pallas_call | solution.py:485
  55.6 0.5 slice.3
  56.1 0.8 %copy.12 = f32[3,144,288]{2,1,0:T(8,128)} copy(f32[3,144,288]{2,1,0:T(8,128)S(1)} %get-tuple-element.13) | data formatting | bytes 995328
  57.0 0.6 %copy.13 = f32[8,1152]{1,0:T(8,128)} copy(f32[8,1152]{1,0:T(8,128)S(1)} %get-tuple-element.14) | data formatting | bytes 73728
Async XLA Ops:
  1.6 0.7 %copy-start = (bf16[8,1152]{1,0:T(8,128)(2,1)S(1)}, bf16[8,1152]{1,0:T(8,128)(2,1)}, u32[]{:S(2)}) copy-start(bf16[8,1152]{1,0:T(8,128)(2,1)} %cap_hbm.1) | copy-start | bytes 55300
  2.4 0.7 %copy-start.1 = (s32[32]{0:T(128)S(1)}, s32[32]{0:T(128)}, u32[]{:S(2)}) copy-start(s32[32]{0:T(128)} %param.7) | copy-start | bytes 388

commit v4 on v3

--- a/solution.py
+++ b/solution.py
@@ -157,6 +157,7 @@
     acc,
     cap_sem,
     pos_sem,
+    own_sem,
     w_sem,
     fr_send,
     fr_recv,
@@ -194,6 +195,8 @@
 
     cap_copy = pltpu.make_async_copy(cap_hbm, cap_ref, cap_sem)
     cap_copy.start()
+    own_copy = pltpu.make_async_copy(frames_ref.at[f], x_rows.at[f], own_sem)
+    own_copy.start()
     pos_copy = pltpu.make_async_copy(pos_hbm, pos_ref, pos_sem)
     pos_copy.start()
     w_copies = [pltpu.make_async_copy(w_hbm.at[k], w_ref.at[k], w_sem.at[k]) for k in range(3)]
@@ -211,6 +214,13 @@
         pl.semaphore_signal(barrier, inc=1, device_id=(cpeer(d), f), device_id_type=MESH)
     for d in range(1, F):
         pl.semaphore_signal(barrier, inc=1, device_id=(c, fpeer(d)), device_id_type=MESH)
+
+    cap_copy.wait()
+    capf = cap_ref[...].astype(jnp.float32)
+    cnorm = jnp.sqrt(jnp.sum(capf * capf, axis=1, keepdims=True) + 1e-06)
+    vunit = capf / cnorm
+    v_own = vunit.astype(jnp.bfloat16)
+    vu[c, f] = pack(v_own.astype(jnp.float32), jnp.zeros((NB, 128), jnp.float32))
     pl.semaphore_wait(barrier, C + F - 2)
 
     sends = []
@@ -254,15 +264,6 @@
                 (c, fpeer(d)),
             )
         )
-    x_rows[f] = frames_ref[f]
-
-    cap_copy.wait()
-    pos_copy.wait()
-    capf = cap_ref[...].astype(jnp.float32)
-    cnorm = jnp.sqrt(jnp.sum(capf * capf, axis=1, keepdims=True) + 1e-06)
-    vunit = capf / cnorm
-    v_own = vunit.astype(jnp.bfloat16)
-    vu[c, f] = pack(v_own.astype(jnp.float32), jnp.zeros((NB, 128), jnp.float32))
     for d in range(1, C):
         go(remote(vu.at[c, f], vu.at[c, f], v1_send.at[d], v1_recv.at[d], (cpeer(d), f)))
 
@@ -271,6 +272,8 @@
         remote(
             x_rows.at[source], x_rows.at[source], fr_send.at[d], fr_recv.at[d], (c, source)
         ).wait_recv()
+    own_copy.wait()
+    pos_copy.wait()
     xf = x_rows[...].reshape(ROWS, D).astype(jnp.float32)
     edge = jnp.zeros((NB, D), jnp.float32)
     before = jnp.concatenate([edge, xf[: ROWS - NB]], axis=0).astype(jnp.bfloat16)
@@ -489,7 +492,7 @@
             jax.ShapeDtypeStruct((3, RC, CC), f32),
             jax.ShapeDtypeStruct((NB, D), f32),
         ),
-        in_specs=[vmem, hbm, hbm, hbm],
+        in_specs=[hbm, hbm, hbm, hbm],
         out_specs=(vmem, vmem, vmem),
         scratch_shapes=[
             pltpu.VMEM((NB, D), bf16),
@@ -509,6 +512,7 @@
             pltpu.VMEM((3 * RC, CC), f32),
             dma,
             dma,
+            dma,
             dma((3,)),
             dma((F,)),
             dma((F,)),
@@ -530,7 +534,7 @@
             dma((2, half, F)),
         ],
         compiler_params=pltpu.CompilerParams(
-            collective_id=0, has_side_effects=True, vmem_limit_bytes=52 * 1024 * 1024
+            collective_id=0, has_side_effects=True, vmem_limit_bytes=60 * 1024 * 1024
         ),
         cost_estimate=pl.CostEstimate(
             flops=4 * 3 * ROWS * D * D, bytes_accessed=8 * D * D, transcendentals=ROWS * D

time: 57.8 us -> 60.4 us (1.045)
  local copies, waits for them, and re-layouts: 4.33 us -> 6.26 us
  Pallas kernels: 52.6 us -> 53.3 us
    reshape x1, local copies, waits for them, and re-layouts: 0.99 us -> 1.71 us  [fused(): frames.reshape(F, NB, fr_dev, D).transpose(0, 2, 1, 3)]
    slice x1, local copies, waits for them, and re-layouts: 0.51 us -> 1.2 us  [fused(): return (loss[0, 0], grad_weight, grad_captions)]
    pallas_call x1, Pallas kernels: 52.6 us -> 53.3 us  [fused(): pl.pallas_call(functools.partial(fused_kernel, C, F), out_shape=(jax.Shap...]
    unnamed x6 -> x2, local copies, waits for them, and re-layouts: 2.83 us -> 3.36 us
where the time goes in v4:
time: 60.4 us; the launch traced here: 60.2 us
  Pallas kernels  53.3 us (88%)
  local copies, waits for them, and re-layouts  6.26 us (10%)
  between operations  0.64 us (1%)
    pallas_call x1, Pallas kernels, fused(): pl.pallas_call(functools.partial(fused_kernel, C, F), out_shape=(jax.Shap...  53.3 us
    unnamed x2, local copies, waits for them, and re-layouts  3.36 us
    reshape x1, local copies, waits for them, and re-layouts, fused(): frames.reshape(F, NB, fr_dev, D).transpose(0, 2, 1, 3)  1.71 us

profile of v4, /device:TPU:0, one launch (start us, length us, event | category | flops | bytes accessed | tf_op | source)
XLA Modules:
  0.0 60.2 jit_solution(1671414662576279645)
XLA Ops:
  0.6 1.7 %copy.9 = bf16[4,8,4,1152]{3,1,2,0:T(8,128)(2,1)} copy(bf16[4,8,4,1152]{3,2,1,0:T(4,128)(2,1)} %bitcast.9) | data formatting | bytes 589824 | tf_op jit(solution)/shard_map/reshape | solution.py:482
  2.3 53.3 %shard_map.67 = (f32[8,128]{1,0:T(8,128)}, f32[3,144,288]{2,1,0:T(8,128)}, f32[8,1152]{1,0:T(8,128)}) custom-call(bf16[4,32,1152]{2,1,0:T(8,128)(2,1)} %bitcast.8, bf16[3,1152,1152]{2,1,0:T(8,128)(2,1)} %w_hbm.1, bf16[8,1152]{1,0:T(8,128)(2,1)} %cap_hbm.1, s32[1,32]{1,0:T(1,128)} %bitcast.10), custom_call_target="tpu_custom_call" | custom-call | flops 2038431744 | bytes 10616832 | tf_op jit(solution)/shard_map/pallas_call | solution.py:488
  55.6 1.2 %slice.3 = f32[1,1]{1,0:T(1,128)} slice(f32[8,128]{1,0:T(8,128)} %get-tuple-element.6), slice={[0:1], [0:1]} | slice | bytes 8 | tf_op jit(solution)/shard_map/slice | solution.py:543
  56.8 2.0 %copy.12 = f32[3,144,288]{2,1,0:T(8,128)} copy(f32[3,144,288]{2,1,0:T(8,128)} %get-tuple-element.13) | data formatting | bytes 995328
  58.8 1.4 %copy.13 = f32[8,1152]{1,0:T(8,128)} copy(f32[8,1152]{1,0:T(8,128)} %get-tuple-element.14) | data formatting | bytes 73728

commit v5 on v4

--- a/solution.py
+++ b/solution.py
@@ -319,9 +319,6 @@
     for d in range(1, C):
         go(remote(uu.at[c, f], uu.at[c, f], u1_send.at[d], u1_recv.at[d], (cpeer(d), f)))
 
-    clip_arrive(xu, x1_send, x1_recv)
-    spread(xu, x2_send, x2_recv)
-
     spread_end(vu, v2_send, v2_recv)
     caps = C * F * NB
     vb[...] = unpack(vu[...], D)[0]
@@ -398,8 +395,14 @@
             if q in units_at(way, 1):
                 forward(way, 0, q)
 
+    clip_arrive(xu, x1_send, x1_recv)
+    spread(xu, x2_send, x2_recv)
     relay(1, 0)
+    clip_arrive(uu, u1_send, u1_recv)
+    spread(uu, u2_send, u2_recv)
+    relay(1, 1, 2)
     spread_on(xu, x2_send, x2_recv)
+    relay(1, 3)
     spread_end(xu, x2_send, x2_recv)
     row = lax.broadcasted_iota(jnp.int32, (ROWS, ROWS), 0)
     col = lax.broadcasted_iota(jnp.int32, (ROWS, ROWS), 1)
@@ -421,28 +424,19 @@
         return carry
 
     quarter = C // 4
-    lax.fori_loop(0, quarter, shift, 0)
-    relay(1, 1)
-    lax.fori_loop(quarter, 2 * quarter, shift, 0)
-    relay(1, 2)
-    lax.fori_loop(2 * quarter, 3 * quarter, shift, 0)
-    relay(1, 3)
-    clip_arrive(uu, u1_send, u1_recv)
-    spread(uu, u2_send, u2_recv)
-    lax.fori_loop(3 * quarter, C, shift, 0)
-    relay(2, 0)
+    for q in range(4):
+        lax.fori_loop(q * quarter, (q + 1) * quarter, shift, 0)
+        relay(2, q)
     add_block(c, first=True)
-    relay(2, 1)
+    spread_on(uu, u2_send, u2_recv)
     add_block(block_at(0, 1))
-    relay(2, 2)
+    relay(3, 0)
     add_block(block_at(1, 1))
-    relay(2, 3)
-    spread_on(uu, u2_send, u2_recv)
-    relay(3, 0)
+    relay(3, 1)
     add_block(block_at(0, 2))
-    relay(3, 1)
+    relay(3, 2)
     add_block(block_at(1, 2))
-    relay(3, 2)
+    relay(3, 3)
     spread_end(uu, u2_send, u2_recv)
     u_all, halves = unpack(uu[...], D)
     ub[...] = u_all
@@ -457,7 +451,6 @@
     dv = jnp.dot(coef_own, ub[...], preferred_element_type=jnp.float32)
     gc_ref[...] = (dv - vunit * jnp.sum(vunit * dv, axis=1, keepdims=True)) / cnorm
 
-    relay(3, 3)
     every = 10.0 * nt_dot(ub[...], vb[...]) - 10.0
     all_ids = lax.broadcasted_iota(jnp.int32, (caps, caps), 1).astype(jnp.float32)
     signed = jnp.where(pos_all == all_ids, -every, every)
@@ -534,7 +527,7 @@
             dma((2, half, F)),
         ],
         compiler_params=pltpu.CompilerParams(
-            collective_id=0, has_side_effects=True, vmem_limit_bytes=60 * 1024 * 1024
+            collective_id=0, has_side_effects=True, vmem_limit_bytes=52 * 1024 * 1024
         ),
         cost_estimate=pl.CostEstimate(
             flops=4 * 3 * ROWS * D * D, bytes_accessed=8 * D * D, transcendentals=ROWS * D

time: 60.4 us -> 52.9 us (0.88)
  Pallas kernels: 53.3 us -> 47.7 us
  local copies, waits for them, and re-layouts: 6.26 us -> 4.33 us
    pallas_call x1, Pallas kernels: 53.3 us -> 47.7 us  [fused(): pl.pallas_call(functools.partial(fused_kernel, C, F), out_shape=(jax.Shap...]
    reshape x1, local copies, waits for them, and re-layouts: 1.71 us -> 0.99 us  [fused(): frames.reshape(F, NB, fr_dev, D).transpose(0, 2, 1, 3)]
    slice x1, local copies, waits for them, and re-layouts: 1.2 us -> 0.51 us  [fused(): return (loss[0, 0], grad_weight, grad_captions)]
    unnamed x2 -> x6, local copies, waits for them, and re-layouts: 3.36 us -> 2.83 us
where the time goes in v5:
time: 52.9 us; the launch traced here: 52.7 us
  Pallas kernels  47.7 us (90%)
  local copies, waits for them, and re-layouts  4.33 us (8%)
  between operations  0.65 us (1%)
    pallas_call x1, Pallas kernels, fused(): pl.pallas_call(functools.partial(fused_kernel, C, F), out_shape=(jax.Shap...  47.7 us
    unnamed x6, local copies, waits for them, and re-layouts  2.83 us

profile of v5, /device:TPU:0, one launch (start us, length us, event | category | flops | bytes accessed | tf_op | source)
XLA Modules:
  0.0 52.7 jit_solution(10035618176807526690)
XLA Ops:
  0.6 1.0 %copy.9 = bf16[4,8,4,1152]{3,1,2,0:T(8,128)(2,1)S(1)} copy(bf16[4,8,4,1152]{3,2,1,0:T(4,128)(2,1)} %bitcast.10) | data formatting | bytes 589824 | tf_op jit(solution)/shard_map/reshape | solution.py:475
  1.6 0.0 copy-start
  1.6 0.7 %copy-done = bf16[8,1152]{1,0:T(8,128)(2,1)S(1)} copy-done((bf16[8,1152]{1,0:T(8,128)(2,1)S(1)}, bf16[8,1152]{1,0:T(8,128)(2,1)}, u32[]{:S(2)}) %copy-start) | copy-done | bytes 18456
  2.4 0.0 copy-start.1
  2.4 0.7 %copy-done.1 = s32[32]{0:T(128)S(1)} copy-done((s32[32]{0:T(128)S(1)}, s32[32]{0:T(128)}, u32[]{:S(2)}) %copy-start.1) | copy-done | bytes 152
  3.0 47.7 %shard_map.67 = (f32[8,128]{1,0:T(8,128)S(1)}, f32[3,144,288]{2,1,0:T(8,128)S(1)}, f32[8,1152]{1,0:T(8,128)S(1)}) custom-call(bf16[4,32,1152]{2,1,0:T(8,128)(2,1)S(1)} %bitcast.8, bf16[3,1152,1152]{2,1,0:T(8,128)(2,1)} %w_hbm.1, bf16[8,1152]{1,0:T(8,128)(2,1)S(1)} %copy-done, s32[1,32]{1,0:T(1,128)S(1)} %bitcast.9), custom_call_target="tpu_custom_call" | custom-call | flops 2038431744 | bytes 10616832 | tf_op jit(solution)/shard_map/pallas_call | solution.py:481
  50.7 0.5 slice.3
  51.2 0.8 %copy.12 = f32[3,144,288]{2,1,0:T(8,128)} copy(f32[3,144,288]{2,1,0:T(8,128)S(1)} %get-tuple-element.13) | data formatting | bytes 995328
  52.1 0.6 %copy.13 = f32[8,1152]{1,0:T(8,128)} copy(f32[8,1152]{1,0:T(8,128)S(1)} %get-tuple-element.14) | data formatting | bytes 73728
Async XLA Ops:
  1.6 0.7 %copy-start = (bf16[8,1152]{1,0:T(8,128)(2,1)S(1)}, bf16[8,1152]{1,0:T(8,128)(2,1)}, u32[]{:S(2)}) copy-start(bf16[8,1152]{1,0:T(8,128)(2,1)} %cap_hbm.1) | copy-start | bytes 55300
  2.4 0.7 %copy-start.1 = (s32[32]{0:T(128)S(1)}, s32[32]{0:T(128)}, u32[]{:S(2)}) copy-start(s32[32]{0:T(128)} %param.7) | copy-start | bytes 388

commit v6 on v5

--- a/solution.py
+++ b/solution.py
@@ -279,6 +279,8 @@
     before = jnp.concatenate([edge, xf[: ROWS - NB]], axis=0).astype(jnp.bfloat16)
     after = jnp.concatenate([xf[NB:], edge], axis=0).astype(jnp.bfloat16)
     w_copies[0].wait()
+    clip_arrive(vu, v1_send, v1_recv)
+    spread(vu, v2_send, v2_recv)
     conv = jnp.dot(before, w_ref[0], preferred_element_type=jnp.float32)
     xt[...] = xf.T.astype(jnp.bfloat16).reshape(C, RC, ROWS)
     for d in range(1, C):
@@ -286,17 +288,13 @@
         go(remote(xt.at[to], xu.at[c, f], x1_send.at[d], x1_recv.at[d], (to, f)))
     xu[c, f] = xt[c]
 
-    clip_arrive(vu, v1_send, v1_recv)
-    spread(vu, v2_send, v2_recv)
-
     w_copies[1].wait()
     conv = conv + jnp.dot(
         x_rows[...].reshape(ROWS, D), w_ref[1], preferred_element_type=jnp.float32
     )
+    spread_on(vu, v2_send, v2_recv)
     w_copies[2].wait()
     conv = conv + jnp.dot(after, w_ref[2], preferred_element_type=jnp.float32)
-
-    spread_on(vu, v2_send, v2_recv)
 
     scale = math.sqrt(2.0 / math.pi)
     square = conv * conv
@@ -331,9 +329,10 @@
     step = dpooled * (1.0 / T)
     dconv = (slope[...].reshape(T, NB, D) * step[None]).reshape(ROWS, D)
     dt[...] = dconv.T.astype(jnp.bfloat16).reshape(F, CC, ROWS)
-    for d in range(1, F):
-        to = fpeer(d)
-        go(remote(dt.at[to], dbuf.at[c, f], da_send.at[d], da_recv.at[d], (c, to)))
+    family = (f, beside, across, diagonal)
+    for q in (2, 3, 1):
+        to = family[q]
+        go(remote(dt.at[to], dbuf.at[c, f], da_send.at[q], da_recv.at[q], (c, to)))
     dbuf[c, f] = dt[f]
 
     ways = (right, left)
@@ -347,7 +346,7 @@
         return range(F // 2) if way == 0 else range(F // 2, F)
 
     def forward(way, hop, q):
-        slot = dbuf.at[block_at(way, hop), fpeer(F - q)]
+        slot = dbuf.at[block_at(way, hop), family[q]]
         go(
             remote(
                 slot,
@@ -359,7 +358,7 @@
         )
 
     def arrive(way, hop, q):
-        slot = dbuf.at[block_at(way, hop), fpeer(F - q)]
+        slot = dbuf.at[block_at(way, hop), family[q]]
         remote(
             slot,
             slot,
@@ -388,7 +387,7 @@
 
     for q in range(F):
         if q:
-            source = fpeer(F - q)
+            source = family[q]
             slot = dbuf.at[c, source]
             remote(slot, slot, da_send.at[q], da_recv.at[q], (c, source)).wait_recv()
         for way in range(2):

time: 52.9 us -> 52.8 us (level)
  no operation moved by 1% of the time
where the time goes in v6:
time: 52.8 us; the launch traced here: 52.6 us
  Pallas kernels  47.6 us (90%)
  local copies, waits for them, and re-layouts  4.33 us (8%)
  between operations  0.65 us (1%)
    pallas_call x1, Pallas kernels, fused(): pl.pallas_call(functools.partial(fused_kernel, C, F), out_shape=(jax.Shap...  47.6 us
    unnamed x6, local copies, waits for them, and re-layouts  2.83 us

profile of v6, /device:TPU:0, one launch (start us, length us, event | category | flops | bytes accessed | tf_op | source)
XLA Modules:
  0.0 52.6 jit_solution(16856816145253989965)
XLA Ops:
  0.6 1.0 %copy.9 = bf16[4,8,4,1152]{3,1,2,0:T(8,128)(2,1)S(1)} copy(bf16[4,8,4,1152]{3,2,1,0:T(4,128)(2,1)} %bitcast.10) | data formatting | bytes 589824 | tf_op jit(solution)/shard_map/reshape | solution.py:474
  1.6 0.0 copy-start
  1.6 0.7 %copy-done = bf16[8,1152]{1,0:T(8,128)(2,1)S(1)} copy-done((bf16[8,1152]{1,0:T(8,128)(2,1)S(1)}, bf16[8,1152]{1,0:T(8,128)(2,1)}, u32[]{:S(2)}) %copy-start) | copy-done | bytes 18456
  2.4 0.0 copy-start.1
  2.4 0.7 %copy-done.1 = s32[32]{0:T(128)S(1)} copy-done((s32[32]{0:T(128)S(1)}, s32[32]{0:T(128)}, u32[]{:S(2)}) %copy-start.1) | copy-done | bytes 152
  3.0 47.6 %shard_map.67 = (f32[8,128]{1,0:T(8,128)S(1)}, f32[3,144,288]{2,1,0:T(8,128)S(1)}, f32[8,1152]{1,0:T(8,128)S(1)}) custom-call(bf16[4,32,1152]{2,1,0:T(8,128)(2,1)S(1)} %bitcast.8, bf16[3,1152,1152]{2,1,0:T(8,128)(2,1)} %w_hbm.1, bf16[8,1152]{1,0:T(8,128)(2,1)S(1)} %copy-done, s32[1,32]{1,0:T(1,128)S(1)} %bitcast.9), custom_call_target="tpu_custom_call" | custom-call | flops 2038431744 | bytes 10616832 | tf_op jit(solution)/shard_map/pallas_call | solution.py:480
  50.6 0.5 slice.3
  51.1 0.8 %copy.12 = f32[3,144,288]{2,1,0:T(8,128)} copy(f32[3,144,288]{2,1,0:T(8,128)S(1)} %get-tuple-element.13) | data formatting | bytes 995328
  52.0 0.6 %copy.13 = f32[8,1152]{1,0:T(8,128)} copy(f32[8,1152]{1,0:T(8,128)S(1)} %get-tuple-element.14) | data formatting | bytes 73728
Async XLA Ops:
  1.6 0.7 %copy-start = (bf16[8,1152]{1,0:T(8,128)(2,1)S(1)}, bf16[8,1152]{1,0:T(8,128)(2,1)}, u32[]{:S(2)}) copy-start(bf16[8,1152]{1,0:T(8,128)(2,1)} %cap_hbm.1) | copy-start | bytes 55300
  2.4 0.7 %copy-start.1 = (s32[32]{0:T(128)S(1)}, s32[32]{0:T(128)}, u32[]{:S(2)}) copy-start(s32[32]{0:T(128)} %param.7) | copy-start | bytes 388

commit v7 on v6

--- a/solution.py
+++ b/solution.py
@@ -386,6 +386,9 @@
             acc[...] += block_term(block)
 
     for q in range(F):
+        if q == 2:
+            clip_arrive(xu, x1_send, x1_recv)
+            spread(xu, x2_send, x2_recv)
         if q:
             source = family[q]
             slot = dbuf.at[c, source]
@@ -394,14 +397,12 @@
             if q in units_at(way, 1):
                 forward(way, 0, q)
 
-    clip_arrive(xu, x1_send, x1_recv)
-    spread(xu, x2_send, x2_recv)
     relay(1, 0)
     clip_arrive(uu, u1_send, u1_recv)
     spread(uu, u2_send, u2_recv)
-    relay(1, 1, 2)
+    relay(1, 1)
     spread_on(xu, x2_send, x2_recv)
-    relay(1, 3)
+    relay(1, 2, 3)
     spread_end(xu, x2_send, x2_recv)
     row = lax.broadcasted_iota(jnp.int32, (ROWS, ROWS), 0)
     col = lax.broadcasted_iota(jnp.int32, (ROWS, ROWS), 1)

time: 52.8 us -> 52.4 us (level)
  no operation moved by 1% of the time
where the time goes in v7:
time: 52.4 us; the launch traced here: 52.2 us
  Pallas kernels  47.2 us (90%)
  local copies, waits for them, and re-layouts  4.33 us (8%)
  between operations  0.65 us (1%)
    pallas_call x1, Pallas kernels, fused(): pl.pallas_call(functools.partial(fused_kernel, C, F), out_shape=(jax.Shap...  47.2 us
    unnamed x6, local copies, waits for them, and re-layouts  2.83 us

profile of v7, /device:TPU:0, one launch (start us, length us, event | category | flops | bytes accessed | tf_op | source)
XLA Modules:
  0.0 52.2 jit_solution(6671001399740794749)
XLA Ops:
  0.6 1.0 %copy.9 = bf16[4,8,4,1152]{3,1,2,0:T(8,128)(2,1)S(1)} copy(bf16[4,8,4,1152]{3,2,1,0:T(4,128)(2,1)} %bitcast.10) | data formatting | bytes 589824 | tf_op jit(solution)/shard_map/reshape | solution.py:475
  1.6 0.0 copy-start
  1.6 0.7 %copy-done = bf16[8,1152]{1,0:T(8,128)(2,1)S(1)} copy-done((bf16[8,1152]{1,0:T(8,128)(2,1)S(1)}, bf16[8,1152]{1,0:T(8,128)(2,1)}, u32[]{:S(2)}) %copy-start) | copy-done | bytes 18456
  2.4 0.0 copy-start.1
  2.4 0.7 %copy-done.1 = s32[32]{0:T(128)S(1)} copy-done((s32[32]{0:T(128)S(1)}, s32[32]{0:T(128)}, u32[]{:S(2)}) %copy-start.1) | copy-done | bytes 152
  3.0 47.2 %shard_map.67 = (f32[8,128]{1,0:T(8,128)S(1)}, f32[3,144,288]{2,1,0:T(8,128)S(1)}, f32[8,1152]{1,0:T(8,128)S(1)}) custom-call(bf16[4,32,1152]{2,1,0:T(8,128)(2,1)S(1)} %bitcast.8, bf16[3,1152,1152]{2,1,0:T(8,128)(2,1)} %w_hbm.1, bf16[8,1152]{1,0:T(8,128)(2,1)S(1)} %copy-done, s32[1,32]{1,0:T(1,128)S(1)} %bitcast.9), custom_call_target="tpu_custom_call" | custom-call | flops 2038431744 | bytes 10616832 | tf_op jit(solution)/shard_map/pallas_call | solution.py:481
  50.3 0.5 slice.3
  50.8 0.8 %copy.12 = f32[3,144,288]{2,1,0:T(8,128)} copy(f32[3,144,288]{2,1,0:T(8,128)S(1)} %get-tuple-element.13) | data formatting | bytes 995328
  51.6 0.6 %copy.13 = f32[8,1152]{1,0:T(8,128)} copy(f32[8,1152]{1,0:T(8,128)S(1)} %get-tuple-element.14) | data formatting | bytes 73728
Async XLA Ops:
  1.6 0.7 %copy-start = (bf16[8,1152]{1,0:T(8,128)(2,1)S(1)}, bf16[8,1152]{1,0:T(8,128)(2,1)}, u32[]{:S(2)}) copy-start(bf16[8,1152]{1,0:T(8,128)(2,1)} %cap_hbm.1) | copy-start | bytes 55300
  2.4 0.7 %copy-start.1 = (s32[32]{0:T(128)S(1)}, s32[32]{0:T(128)}, u32[]{:S(2)}) copy-start(s32[32]{0:T(128)} %param.7) | copy-start | bytes 388
